TPU v7x, 32 devices: a whole 2x2x4 slice. The times are simulated.
32 devices in a mesh: section: 4 (over y, core), dp: 8 (over z, x).
Axes of the slice: x: 2, y: 2, z: 4, core: 2. Of those that a mesh axis runs over, the one named last changes fastest.
Arguments:
- latents: bfloat16 [6, 176, 1536], P(None, 'dp'), may hold values from -6 to 6
- control_hint: bfloat16 [6, 176, 1536], P(None, 'dp'), may hold values from -6 to 6
- upstream: bfloat16 [6, 176, 1536], P(None, 'dp'), may hold values from -6 to 6
- batch_order: int32 [6], replicated, may hold values from 0 to 5, each once
- section_weight: bfloat16 [4, 1536, 1536], P('section'), may hold values from -0.078125 to 0.078125
- zero_weight: bfloat16 [4, 768, 1536], P('section'), may hold values from -0.0390625 to 0.0390625
Outputs:
- zero_grad: float32 [4, 768, 1536], P('section', 'dp')
Inputs may be any that keep to these rules, and one draw needn't show every extreme that they name: batch_order names each of the 6 micro-batches exactly once.
All inputs are finite; a program needn't handle non-finite values.
Results may differ from a plain program's by a relative error of at most 0.03.
Values may be sent and summed in bfloat16 or wider, within the bound.
A program may use at most 64 MiB of HBM per device.

v0:
```python
import functools
import math

import jax
import jax.numpy as jnp
from jax import lax
from jax.experimental import pallas as pl
from jax.experimental.pallas import tpu as pltpu
from jax.sharding import PartitionSpec as P

tanh_coef = 0.7978845608028654
cube_coef = 0.044715
f32 = jnp.float32
bf16 = jnp.bfloat16


def gelu_parts(values):
    square = values * values
    tangent = jnp.tanh(tanh_coef * (values + cube_coef * square * values))
    return square, tangent


def gelu_value(values):
    _, tangent = gelu_parts(values)
    return 0.5 * values * (1.0 + tangent)


def gelu_slope(values):
    square, tangent = gelu_parts(values)
    return 0.5 * (1.0 + tangent) + 0.5 * values * (1.0 - tangent * tangent) * tanh_coef * (
        1.0 + 3.0 * cube_coef * square
    )


def mm(left, right):
    return jnp.dot(left, right, preferred_element_type=f32)


def kernel(
    blocks, n_dp, order_any, lat_any, hint_any, up_any, w_any, z_any, out_ref,
    order, lat, hint, up, w, z, flat, chain, mine, side, hside, resid, pout, back, slope, gbuf,
    other, rside, et, ecol, acc, sent, ret, load_sem, chain_s, chain_r, side_s, side_r, resid_s, resid_r,
    back_s, back_r, e_s, e_r, ag_s, ag_r, sib_s, sib_r, ret_s, ret_r, rside_s, rside_r,
):
    sections = 2 * blocks
    line = n_dp // 2
    early = min(1, line - 1)
    micro, rows, width = lat.shape
    half = width // 2
    padded = flat.shape[0]
    share = ret.shape[0]
    lanes = et.shape[3]
    extra = padded - lanes
    place = lax.axis_index("section")
    me = lax.axis_index("dp")
    depth = place // 2
    parity = place % 2
    sibling = place + 1 - 2 * parity
    here, across = me // 2, me % 2
    partner = me + 1 - 2 * across
    is_base = parity == 0
    is_control = parity == 1
    first = depth == 0
    last = depth == blocks - 1
    aide = depth == blocks - 2
    active = (True, depth > 0, aide)
    cuts = [slice(0, half), slice(half, width)]

    when = pl.when
    loads = [
        (first, pltpu.make_async_copy(order_any, order, load_sem.at[0])),
        (first, pltpu.make_async_copy(lat_any, lat, load_sem.at[1])),
        (first & is_control, pltpu.make_async_copy(hint_any, hint, load_sem.at[2])),
        (depth >= blocks - 2, pltpu.make_async_copy(up_any, up, load_sem.at[3])),
    ]
    load_w = pltpu.make_async_copy(w_any.at[0], w, load_sem.at[4])
    load_z = pltpu.make_async_copy(z_any.at[0], z, load_sem.at[5])
    for needed, load in loads:

        @when(needed)
        def _():
            load.start()

    load_w.start()
    load_z.start()

    barrier = pltpu.get_barrier_semaphore()

    def greet(step, carry):
        pl.semaphore_signal(
            barrier, inc=1, device_id={"dp": lax.rem(me + step, n_dp)},
            device_id_type=pl.DeviceIdType.MESH,
        )
        return carry

    lax.fori_loop(1, n_dp, greet, 0)
    greeted = n_dp - 1
    for step in (-3, -2, -1, 1, 2, 3):
        there = place + step
        inside = (there >= 0) & (there < sections)

        @when(inside)
        def _():
            pl.semaphore_signal(
                barrier, inc=1, device_id={"section": there}, device_id_type=pl.DeviceIdType.MESH
            )

        greeted = greeted + jnp.where(inside, 1, 0)

    def remote(src, dst, send, recv, **where):
        return pltpu.make_async_remote_copy(
            src_ref=src, dst_ref=dst, send_sem=send, recv_sem=recv, device_id=where,
            device_id_type=pl.DeviceIdType.MESH,
        )

    for needed, load in loads:

        @when(needed)
        def _():
            load.wait()

    def fill(slot_rows, targets):
        flat[padded - 16 :, :] = jnp.zeros((16, width), f32)
        for slot in range(micro):
            flat[slot * rows : (slot + 1) * rows, :] = slot_rows(slot)
        for part in range(2):
            if targets[part] is not None:
                targets[part][...] = flat[:, cuts[part]].astype(bf16)

    @when(last)
    def _():
        fill(lambda slot: up[slot].astype(f32), [gbuf.at[0, me], other])

    @when(aide)
    def _():
        fill(lambda slot: up[slot].astype(f32), [None, gbuf.at[2, me]])

    def fill_first(slot_rows):
        fill(slot_rows, [chain.at[0], chain.at[1]])

    @when(first & is_base)
    def _():
        fill_first(lambda slot: lat[order[slot]].astype(f32))

    @when(first & is_control)
    def _():
        fill_first(lambda slot: lat[order[slot]].astype(f32) + hint[order[slot]].astype(f32))

    pl.semaphore_wait(barrier, greeted)

    def hop(stream, d, way, **where):
        return remote(
            gbuf.at[stream, d], gbuf.at[stream, d],
            ag_s.at[3 * stream + way, d], ag_r.at[stream, d], **where,
        )

    def go_up(stream, d):
        return hop(stream, d, 0, dp=me + 2)

    def go_down(stream, d):
        return hop(stream, d, 1, dp=me - 2)

    def go_across(stream, d):
        return hop(stream, d, 2, dp=partner)

    def go_sibling(stream, d):
        return remote(
            gbuf.at[stream, d], gbuf.at[stream, d], sib_s.at[stream, d], sib_r.at[stream, d], section=sibling
        )

    def gather_start(stream):
        @when(here + 1 < line)
        def _():
            go_up(stream, me).start()

        @when(here > 0)
        def _():
            go_down(stream, me).start()

        go_across(stream, me).start()

    def forward(stream, reach):
        @when(here - reach >= 0)
        def _():
            d = me - 2 * reach
            hop(stream, d, 2, dp=partner).wait_recv()

            @when(here + 1 < line)
            def _():
                go_up(stream, d).start()

            go_across(stream, d).start()
            go_sibling(stream, d).start()

        @when(here + reach < line)
        def _():
            d = me + 2 * reach
            hop(stream, d, 2, dp=partner).wait_recv()

            @when(here > 0)
            def _():
                go_down(stream, d).start()

            go_across(stream, d).start()
            go_sibling(stream, d).start()

    def sides(near, job):
        @when(here - near >= 0)
        def _():
            job(-2 * near)

        @when((here + near < line) & (near > 0))
        def _():
            job(2 * near)

    def cross(stream, near):
        def job(shift):
            d = partner + shift
            hop(stream, d, 2, dp=partner).wait_recv()
            go_sibling(stream, d).start()

        sides(near, job)

    def finish(stream, near):
        def job(shift):
            for d in (me + shift, partner + shift):
                if stream == 0:
                    given = is_base & ((d != me) | (first & jnp.logical_not(last)))
                elif stream == 1:
                    given = is_control
                else:
                    given = is_control & (d != me)

                @when(given)
                def _():
                    go_sibling(stream, d).wait_recv()

                @when(d != me)
                def _():
                    remote(
                        et.at[stream, d], ecol.at[stream, d], e_s.at[stream, 0],
                        e_r.at[stream, d], dp=partner,
                    ).wait_recv()

                term = mm(ecol[stream, d, extra:, :], gbuf[stream, d, :lanes, :])
                rest = ecol[stream, d, :extra, :].astype(f32).T[:share, :].astype(bf16)
                acc[stream] += term + mm(rest, gbuf[stream, d, lanes:, :])

        sides(near, job)

    def loop(low, high, step):
        def once(index, carry):
            step(index)
            return carry

        lax.fori_loop(low, high, once, 0)

    def gather_loop(stream):
        def step(reach):
            forward(stream, reach)
            cross(stream, reach - 1)
            finish(stream, reach - 1)

        loop(1, line + 1, step)

    def finish_loop(stream):
        loop(0, line, lambda near: finish(stream, near))

    @when(last & is_control)
    def _():
        gather_start(0)

    @when(aide & is_base)
    def _():
        gather_start(2)

    acc[...] = jnp.zeros_like(acc)
    et[...] = jnp.zeros_like(et)
    load_w.wait()

    def to_chain(part, target=None):
        target = place + 2 if target is None else target
        return remote(mine.at[part], chain.at[part], chain_s.at[part], chain_r.at[part], section=target)

    def to_side(target):
        return remote(mine.at[0], side, side_s.at[0], side_r.at[0], section=target)

    def to_hside(target):
        return remote(chain.at[0], hside, side_s.at[1], side_r.at[1], section=target)

    def to_resid(part, target):
        return remote(pout.at[part], resid.at[part], resid_s.at[part], resid_r.at[part], section=target)

    def to_back(target):
        return remote(back, gbuf.at[0, me], back_s.at[0], back_r.at[0], section=target)

    def to_earlier(target):
        return remote(gbuf.at[1, me], other, back_s.at[1], back_r.at[1], section=target)

    def to_aide(part, target):
        return remote(mine.at[part], rside, rside_s.at[part], rside_r, section=target)

    def to_return(stream, target):
        return remote(sent.at[stream - 1], ret, ret_s.at[stream - 1], ret_r, section=target)

    def give_back(stream, target):
        sent[stream - 1] = acc[stream].astype(bf16)
        to_return(stream, target).start()

    def spread(group, columns):
        wide = columns.astype(f32)
        turned = wide[:lanes, :].T
        for d in range(n_dp):
            mine_rows = slice(d * share, (d + 1) * share)
            et[group, d, :extra, :share] = wide[lanes:, mine_rows].astype(bf16)
            et[group, d, extra:, :] = turned[mine_rows, :].astype(bf16)
        ecol[group, me] = et[group, me]

        def send(step):
            there = lax.rem(me + step, n_dp)
            remote(
                et.at[group, there], ecol.at[group, me], e_s.at[group, step], e_r.at[group, me], dp=there
            ).start()

        loop(1, n_dp, send)

    @when(last & is_control)
    def _():
        for reach in range(1, early + 1):
            forward(0, reach)

    @when(is_control)
    def _():
        @when(depth > 0)
        def _():
            to_chain(0, sibling).wait_recv()
            to_hside(sibling).start()
            to_chain(1, sibling).wait_recv()

        for part in range(2):
            value = mm(chain[0], w[:half, cuts[part]]) + mm(chain[1], w[half:, cuts[part]])
            mine[part] = (chain[part].astype(f32) + gelu_value(value)).astype(bf16)
            if part == 0:
                to_side(place - 1).start()

            @when(jnp.logical_not(last))
            def _():
                to_chain(part).start()

            @when(last)
            def _():
                to_aide(part, place - 3 + part).start()

        load_z.wait()

        @when(jnp.logical_not(last))
        def _():
            for part in range(2):
                pout[part] = mm(mine[1], z[:, cuts[part]]).astype(bf16)
                to_resid(part, place - 1).start()

        @when(depth > 0)
        def _():
            spread(1, chain[1])

        spread(0, mine[1])

        @when(jnp.logical_not(last))
        def _():
            to_back(sibling).wait_recv()
            gather_start(0)
            go_sibling(0, me).start()

        @when(aide)
        def _():
            to_aide(1, sibling).wait_recv()
            spread(2, rside[...])
            finish_loop(2)
            give_back(2, place + 2)

        @when(jnp.logical_not(last))
        def _():
            gather_loop(0)

        @when(last)
        def _():
            loop(early + 1, line, lambda reach: forward(0, reach))
            loop(0, line, lambda near: cross(0, near))
            finish_loop(0)

        @when(depth > 0)
        def _():
            finish_loop(1)
            give_back(1, place - 2)

    @when(is_base)
    def _():
        @when(depth > 0)
        def _():
            to_hside(sibling).wait_recv()
            spread(1, hside[...])
            to_chain(0, sibling).wait_recv()

        slope[...] = mm(chain[0], w[:half, :])

        @when(last)
        def _():
            to_side(sibling).wait_recv()
            spread(0, side[...])

        @when(depth > 0)
        def _():
            to_chain(1, sibling).wait_recv()

        for part in range(2):
            value = slope[:, cuts[part]] + mm(chain[1], w[half:, cuts[part]])

            @when(depth > 0)
            def _():
                slope[:, cuts[part]] = gelu_slope(value)

            @when(jnp.logical_not(last))
            def _():
                flat[:, cuts[part]] = chain[part].astype(f32) + gelu_value(value)

        load_z.wait()

        @when(jnp.logical_not(last))
        def _():
            to_side(sibling).wait_recv()
            for part in range(2):
                flat[:, cuts[part]] += mm(side[...], z[:, cuts[part]])
            for part in range(2):
                to_resid(part, sibling).wait_recv()
                mine[part] = (flat[:, cuts[part]] + resid[part].astype(f32)).astype(bf16)
                to_chain(part).start()

        @when(first & jnp.logical_not(last))
        def _():
            spread(0, side[...])

        @when(aide)
        def _():
            loop(1, line, lambda reach: forward(2, reach))
            loop(0, line, lambda near: cross(2, near))
            to_aide(0, sibling).wait_recv()
            spread(2, rside[...])
            finish_loop(2)
            give_back(2, place + 2)

        @when(depth > 0)
        def _():
            @when(jnp.logical_not(last))
            def _():
                go_sibling(0, me).wait_recv()
                to_earlier(sibling).wait_recv()

            grads = [gbuf[0, me], other[...]]
            scaled = [
                (grads[part].astype(f32) * slope[:, cuts[part]]).astype(bf16) for part in range(2)
            ]
            for part in range(2):
                term = sum(
                    lax.dot_general(
                        scaled[inner], w[cuts[part], cuts[inner]], (((1,), (1,)), ((), ())),
                        preferred_element_type=f32,
                    )
                    for inner in range(2)
                )
                value = (grads[part].astype(f32) + term).astype(bf16)
                if part == 0:
                    back[...] = value
                    to_back(place - 1).start()
                else:
                    gbuf[1, me] = value
                    gather_start(1)
                    go_sibling(1, me).start()

                    @when(depth > 1)
                    def _():
                        to_earlier(place - 2).start()

        @when(depth > 0)
        def _():
            @when(jnp.logical_not(last))
            def _():
                spread(0, side[...])

            gather_loop(1)
            give_back(1, place - 2)

    @when(is_base)
    def _():
        finish_loop(0)

    @when(is_control)
    def _():
        to_side(place - 1).wait_send()

        @when(last)
        def _():
            for part in range(2):
                to_aide(part, place - 3 + part).wait_send()

        @when(depth > 0)
        def _():
            to_hside(sibling).wait_send()

        @when(jnp.logical_not(last))
        def _():
            for part in range(2):
                to_resid(part, place - 1).wait_send()

    @when(is_base & (depth > 0))
    def _():
        to_back(place - 1).wait_send()

        @when(depth > 1)
        def _():
            to_earlier(place - 2).wait_send()

    @when(jnp.logical_not(last))
    def _():
        for part in range(2):
            to_chain(part).wait_send()

    def drain(d):
        for stream in range(3):

            @when((is_control, is_base, is_base)[stream] & active[stream])
            def _():
                @when(d % 2 == across)
                def _():
                    @when((d <= me) & (here + 1 < line))
                    def _():
                        go_up(stream, d).wait_send()

                    @when((d >= me) & (here > 0))
                    def _():
                        go_down(stream, d).wait_send()

                    go_across(stream, d).wait_send()

                @when((d != me) | (jnp.logical_not(last), True, False)[stream])
                def _():
                    go_sibling(stream, d).wait_send()

            @when((d > 0) & active[stream])
            def _():
                remote(
                    et.at[stream, d], ecol.at[stream, d], e_s.at[stream, d], e_r.at[stream, d], dp=partner
                ).wait_send()

    loop(0, n_dp, drain)

    @when(depth > 0)
    def _():
        to_return(1, place - 2).wait_send()

    @when(aide)
    def _():
        to_return(2, place + 2).wait_send()

    to_return(1, sibling).wait_recv()
    out_ref[:, :half] = acc[0]
    out_ref[:, half:] = ret[...].astype(f32)


def body(blocks, n_dp, latents, control_hint, upstream, batch_order, section_weight, zero_weight):
    micro, rows, width = latents.shape
    half = zero_weight.shape[1]
    share = half // n_dp
    padded = (micro * rows + 15) // 16 * 16
    lanes = padded // 128 * 128
    vmem = pl.BlockSpec(memory_space=pltpu.VMEM)
    whole = pl.BlockSpec(memory_space=pl.ANY)
    dma = pltpu.SemaphoreType.DMA
    summed = pl.pallas_call(
        functools.partial(kernel, blocks, n_dp),
        out_shape=jax.ShapeDtypeStruct((share, width), f32),
        in_specs=[whole] * 6,
        out_specs=vmem,
        scratch_shapes=[
            pltpu.SMEM((micro,), jnp.int32),
            pltpu.VMEM((micro, rows, width), bf16),
            pltpu.VMEM((micro, rows, width), bf16),
            pltpu.VMEM((micro, rows, width), bf16),
            pltpu.VMEM((width, width), bf16),
            pltpu.VMEM((half, width), bf16),
            pltpu.VMEM((padded, width), f32),
            pltpu.VMEM((2, padded, half), bf16),
            pltpu.VMEM((2, padded, half), bf16),
            pltpu.VMEM((padded, half), bf16),
            pltpu.VMEM((padded, half), bf16),
            pltpu.VMEM((2, padded, half), bf16),
            pltpu.VMEM((2, padded, half), bf16),
            pltpu.VMEM((padded, half), bf16),
            pltpu.VMEM((padded, width), f32),
            pltpu.VMEM((3, n_dp, padded, half), bf16),
            pltpu.VMEM((padded, half), bf16),
            pltpu.VMEM((padded, half), bf16),
            pltpu.VMEM((3, n_dp, padded - lanes + share, lanes), bf16),
            pltpu.VMEM((3, n_dp, padded - lanes + share, lanes), bf16),
            pltpu.VMEM((3, share, half), f32),
            pltpu.VMEM((2, share, half), bf16),
            pltpu.VMEM((share, half), bf16),
            dma((6,)), dma((2,)), dma((2,)), dma((2,)), dma((2,)), dma((2,)), dma((2,)),
            dma((2,)), dma((2,)), dma((3, n_dp)), dma((3, n_dp)), dma((9, n_dp)), dma((3, n_dp)),
            dma((3, n_dp)), dma((3, n_dp)), dma((2,)), dma, dma((2,)), dma,
        ],
        compiler_params=pltpu.CompilerParams(
            collective_id=0, has_side_effects=True, vmem_limit_bytes=56 * 1024 * 1024
        ),
    )(batch_order, latents, control_hint, upstream, section_weight, zero_weight)
    grad_scale = 1.0 / math.sqrt(micro * rows * n_dp)
    return summed[None] * grad_scale


def solution(mesh):
    placed = (
        P(None, "dp", None),
        P(None, "dp", None),
        P(None, "dp", None),
        P(),
        P("section", None, None),
        P("section", None, None),
    )
    return jax.shard_map(
        functools.partial(body, mesh.shape["section"] // 2, mesh.shape["dp"]),
        mesh=mesh, in_specs=placed, out_specs=P("section", "dp", None), check_vma=False,
    )
```

profile of v0, /device:TPU:0, one launch (start us, length us, event | category | flops | bytes accessed | tf_op | source)
XLA Modules:
  0.0 52.9 jit_solution(1943004772259884446)
XLA Ops:
  0.0 50.9 %shard_map.64 = f32[96,1536]{1,0:T(8,128)} custom-call(s32[6]{0:T(128)} %order_any.1, bf16[6,22,1536]{2,1,0:T(8,128)(2,1)} %lat_any.1, bf16[6,22,1536]{2,1,0:T(8,128)(2,1)} %hint_any.1, bf16[6,22,1536]{2,1,0:T(8,128)(2,1)} %up_any.1, bf16[1,1536,1536]{2,1,0:T(8,128)(2,1)} %w_any.1, bf16[1,768,1536]{2,1,0:T(8,128)(2,1)} %z_any.1), custom_call_target="tpu_custom_call" | custom-call | tf_op jit(solution)/shard_map/pallas_call | solution.py:578
  50.9 1.9 %multiply_bitcast_fusion = f32[1,96,1536]{2,1,0:T(8,128)} fusion(f32[96,1536]{1,0:T(8,128)} %shard_map.64), kind=kLoop, calls=%fused_computation | loop fusion | flops 147456 | bytes 1179648 | tf_op jit(solution)/shard_map/mul | solution.py:616
where the time goes:
time: 53 us; the launch traced here: 52.9 us
  Pallas kernels  50.9 us (96%)
  other arithmetic  1.93 us (4%)
    pallas_call x1, Pallas kernels, body(): pl.pallas_call(functools.partial(kernel, blocks, n_dp), out_shape=jax.Sha...  50.9 us
    mul x1, other arithmetic, body(): return summed[None] * grad_scale  1.93 us

commit v1 on v0

--- a/solution.py
+++ b/solution.py
@@ -37,8 +37,8 @@
 
 
 def kernel(
-    blocks, n_dp, order_any, lat_any, hint_any, up_any, w_any, z_any, out_ref,
-    order, lat, hint, up, w, z, flat, chain, mine, side, hside, resid, pout, back, slope, gbuf,
+    blocks, n_dp, grad_scale, order_any, lat_any, hint_any, up_any, w_any, z_any, out_ref,
+    order, lat, hint, up, w, wt, z, flat, chain, mine, side, hside, resid, pout, back, slope, gbuf,
     other, rside, et, ecol, acc, sent, ret, load_sem, chain_s, chain_r, side_s, side_r, resid_s, resid_r,
     back_s, back_r, e_s, e_r, ag_s, ag_r, sib_s, sib_r, ret_s, ret_r, rside_s, rside_r,
 ):
@@ -338,7 +338,7 @@
             to_chain(1, sibling).wait_recv()
 
         for part in range(2):
-            value = mm(chain[0], w[:half, cuts[part]]) + mm(chain[1], w[half:, cuts[part]])
+            value = mm(jnp.concatenate([chain[0], chain[1]], axis=1), w[:, cuts[part]])
             mine[part] = (chain[part].astype(f32) + gelu_value(value)).astype(bf16)
             if part == 0:
                 to_side(place - 1).start()
@@ -397,6 +397,9 @@
     def _():
         @when(depth > 0)
         def _():
+            block = 2 * 128
+            for start in range(0, width, block):
+                wt[:, start : start + block] = w[start : start + block, :].T
             to_hside(sibling).wait_recv()
             spread(1, hside[...])
             to_chain(0, sibling).wait_recv()
@@ -460,13 +463,7 @@
                 (grads[part].astype(f32) * slope[:, cuts[part]]).astype(bf16) for part in range(2)
             ]
             for part in range(2):
-                term = sum(
-                    lax.dot_general(
-                        scaled[inner], w[cuts[part], cuts[inner]], (((1,), (1,)), ((), ())),
-                        preferred_element_type=f32,
-                    )
-                    for inner in range(2)
-                )
+                term = mm(jnp.concatenate(scaled, axis=1), wt[:, cuts[part]])
                 value = (grads[part].astype(f32) + term).astype(bf16)
                 if part == 0:
                     back[...] = value
@@ -562,8 +559,8 @@
         to_return(2, place + 2).wait_send()
 
     to_return(1, sibling).wait_recv()
-    out_ref[:, :half] = acc[0]
-    out_ref[:, half:] = ret[...].astype(f32)
+    out_ref[0, :, :half] = acc[0] * grad_scale
+    out_ref[0, :, half:] = ret[...].astype(f32) * grad_scale
 
 
 def body(blocks, n_dp, latents, control_hint, upstream, batch_order, section_weight, zero_weight):
@@ -575,9 +572,10 @@
     vmem = pl.BlockSpec(memory_space=pltpu.VMEM)
     whole = pl.BlockSpec(memory_space=pl.ANY)
     dma = pltpu.SemaphoreType.DMA
-    summed = pl.pallas_call(
-        functools.partial(kernel, blocks, n_dp),
-        out_shape=jax.ShapeDtypeStruct((share, width), f32),
+    grad_scale = 1.0 / math.sqrt(micro * rows * n_dp)
+    return pl.pallas_call(
+        functools.partial(kernel, blocks, n_dp, grad_scale),
+        out_shape=jax.ShapeDtypeStruct((1, share, width), f32),
         in_specs=[whole] * 6,
         out_specs=vmem,
         scratch_shapes=[
@@ -585,6 +583,7 @@
             pltpu.VMEM((micro, rows, width), bf16),
             pltpu.VMEM((micro, rows, width), bf16),
             pltpu.VMEM((micro, rows, width), bf16),
+            pltpu.VMEM((width, width), bf16),
             pltpu.VMEM((width, width), bf16),
             pltpu.VMEM((half, width), bf16),
             pltpu.VMEM((padded, width), f32),
@@ -612,8 +611,6 @@
             collective_id=0, has_side_effects=True, vmem_limit_bytes=56 * 1024 * 1024
         ),
     )(batch_order, latents, control_hint, upstream, section_weight, zero_weight)
-    grad_scale = 1.0 / math.sqrt(micro * rows * n_dp)
-    return summed[None] * grad_scale
 
 
 def solution(mesh):

time: 53 us -> 53 us (level)
  other arithmetic: 1.93 us -> 0 us
  local copies, waits for them, and re-layouts: 0 us -> 1.92 us
    mul x1 -> x0, other arithmetic: 1.93 us -> none  [body(): return summed[None] * grad_scale]
    unnamed x0 -> x1, local copies, waits for them, and re-layouts: none -> 1.92 us
where the time goes in v1:
time: 53 us; the launch traced here: 52.8 us
  Pallas kernels  50.9 us (96%)
  local copies, waits for them, and re-layouts  1.92 us (4%)
    pallas_call x1, Pallas kernels, body(): pl.pallas_call(functools.partial(kernel, blocks, n_dp, grad_scale), out_s...  50.9 us
    unnamed x1, local copies, waits for them, and re-layouts  1.92 us

profile of v1, /device:TPU:0, one launch (start us, length us, event | category | flops | bytes accessed | tf_op | source)
XLA Modules:
  0.0 52.8 jit_solution(16625771657432146828)
XLA Ops:
  0.0 50.9 %shard_map.64 = f32[1,96,1536]{2,1,0:T(8,128)} custom-call(s32[6]{0:T(128)} %order_any.1, bf16[6,22,1536]{2,1,0:T(8,128)(2,1)} %lat_any.1, bf16[6,22,1536]{2,1,0:T(8,128)(2,1)} %hint_any.1, bf16[6,22,1536]{2,1,0:T(8,128)(2,1)} %up_any.1, bf16[1,1536,1536]{2,1,0:T(8,128)(2,1)} %w_any.1, bf16[1,768,1536]{2,1,0:T(8,128)(2,1)} %z_any.1), custom_call_target="tpu_custom_call" | custom-call | tf_op jit(solution)/shard_map/pallas_call | solution.py:576
  50.9 1.9 %copy.8 = f32[1,96,1536]{2,1,0:T(8,128)} copy(f32[1,96,1536]{2,1,0:T(8,128)} %shard_map.64) | data formatting | bytes 1179648

commit v2 on v1

--- a/solution.py
+++ b/solution.py
@@ -65,6 +65,8 @@
     aide = depth == blocks - 2
     active = (True, depth > 0, aide)
     cuts = [slice(0, half), slice(half, width)]
+    quarter = half // 2
+    pieces = [slice(0, quarter), slice(quarter, half)]
 
     when = pl.when
     loads = [
@@ -125,18 +127,20 @@
             flat[slot * rows : (slot + 1) * rows, :] = slot_rows(slot)
         for part in range(2):
             if targets[part] is not None:
-                targets[part][...] = flat[:, cuts[part]].astype(bf16)
+                for piece in range(2):
+                    span = slice(part * half + piece * quarter, part * half + (piece + 1) * quarter)
+                    targets[part](piece)[...] = flat[:, span].astype(bf16)
 
     @when(last)
     def _():
-        fill(lambda slot: up[slot].astype(f32), [gbuf.at[0, me], other])
+        fill(lambda slot: up[slot].astype(f32), [lambda piece: gbuf.at[0, piece, me], lambda piece: other.at[piece]])
 
     @when(aide)
     def _():
-        fill(lambda slot: up[slot].astype(f32), [None, gbuf.at[2, me]])
+        fill(lambda slot: up[slot].astype(f32), [None, lambda piece: gbuf.at[2, piece, me]])
 
     def fill_first(slot_rows):
-        fill(slot_rows, [chain.at[0], chain.at[1]])
+        fill(slot_rows, [lambda piece: chain.at[0, :, pieces[piece]], lambda piece: chain.at[1, :, pieces[piece]]])
 
     @when(first & is_base)
     def _():
@@ -148,61 +152,64 @@
 
     pl.semaphore_wait(barrier, greeted)
 
-    def hop(stream, d, way, **where):
+    def hop(stream, piece, d, way, **where):
         return remote(
-            gbuf.at[stream, d], gbuf.at[stream, d],
-            ag_s.at[3 * stream + way, d], ag_r.at[stream, d], **where,
+            gbuf.at[stream, piece, d], gbuf.at[stream, piece, d],
+            ag_s.at[6 * stream + 2 * way + piece, d], ag_r.at[2 * stream + piece, d], **where,
         )
 
-    def go_up(stream, d):
-        return hop(stream, d, 0, dp=me + 2)
-
-    def go_down(stream, d):
-        return hop(stream, d, 1, dp=me - 2)
-
-    def go_across(stream, d):
-        return hop(stream, d, 2, dp=partner)
-
-    def go_sibling(stream, d):
+    def go_up(stream, piece, d):
+        return hop(stream, piece, d, 0, dp=me + 2)
+
+    def go_down(stream, piece, d):
+        return hop(stream, piece, d, 1, dp=me - 2)
+
+    def go_across(stream, piece, d):
+        return hop(stream, piece, d, 2, dp=partner)
+
+    def go_sibling(stream, piece, d):
         return remote(
-            gbuf.at[stream, d], gbuf.at[stream, d], sib_s.at[stream, d], sib_r.at[stream, d], section=sibling
+            gbuf.at[stream, piece, d], gbuf.at[stream, piece, d],
+            sib_s.at[2 * stream + piece, d], sib_r.at[2 * stream + piece, d], section=sibling,
         )
 
-    def gather_start(stream):
+    def gather_start(stream, piece):
         @when(here + 1 < line)
         def _():
-            go_up(stream, me).start()
+            go_up(stream, piece, me).start()
 
         @when(here > 0)
         def _():
-            go_down(stream, me).start()
-
-        go_across(stream, me).start()
+            go_down(stream, piece, me).start()
+
+        go_across(stream, piece, me).start()
 
     def forward(stream, reach):
-        @when(here - reach >= 0)
-        def _():
-            d = me - 2 * reach
-            hop(stream, d, 2, dp=partner).wait_recv()
-
-            @when(here + 1 < line)
-            def _():
-                go_up(stream, d).start()
-
-            go_across(stream, d).start()
-            go_sibling(stream, d).start()
-
-        @when(here + reach < line)
-        def _():
-            d = me + 2 * reach
-            hop(stream, d, 2, dp=partner).wait_recv()
-
-            @when(here > 0)
-            def _():
-                go_down(stream, d).start()
-
-            go_across(stream, d).start()
-            go_sibling(stream, d).start()
+        for piece in range(2):
+
+            @when(here - reach >= 0)
+            def _():
+                d = me - 2 * reach
+                go_across(stream, piece, d).wait_recv()
+
+                @when(here + 1 < line)
+                def _():
+                    go_up(stream, piece, d).start()
+
+                go_across(stream, piece, d).start()
+                go_sibling(stream, piece, d).start()
+
+            @when(here + reach < line)
+            def _():
+                d = me + 2 * reach
+                go_across(stream, piece, d).wait_recv()
+
+                @when(here > 0)
+                def _():
+                    go_down(stream, piece, d).start()
+
+                go_across(stream, piece, d).start()
+                go_sibling(stream, piece, d).start()
 
     def sides(near, job):
         @when(here - near >= 0)
@@ -216,8 +223,9 @@
     def cross(stream, near):
         def job(shift):
             d = partner + shift
-            hop(stream, d, 2, dp=partner).wait_recv()
-            go_sibling(stream, d).start()
+            for piece in range(2):
+                go_across(stream, piece, d).wait_recv()
+                go_sibling(stream, piece, d).start()
 
         sides(near, job)
 
@@ -233,7 +241,8 @@
 
                 @when(given)
                 def _():
-                    go_sibling(stream, d).wait_recv()
+                    for piece in range(2):
+                        go_sibling(stream, piece, d).wait_recv()
 
                 @when(d != me)
                 def _():
@@ -242,9 +251,10 @@
                         e_r.at[stream, d], dp=partner,
                     ).wait_recv()
 
-                term = mm(ecol[stream, d, extra:, :], gbuf[stream, d, :lanes, :])
+                both = jnp.concatenate([gbuf[stream, 0, d], gbuf[stream, 1, d]], axis=1)
+                term = mm(ecol[stream, d, extra:, :], both[:lanes, :])
                 rest = ecol[stream, d, :extra, :].astype(f32).T[:share, :].astype(bf16)
-                acc[stream] += term + mm(rest, gbuf[stream, d, lanes:, :])
+                acc[stream] += term + mm(rest, both[lanes:, :])
 
         sides(near, job)
 
@@ -268,11 +278,13 @@
 
     @when(last & is_control)
     def _():
-        gather_start(0)
+        for piece in range(2):
+            gather_start(0, piece)
 
     @when(aide & is_base)
     def _():
-        gather_start(2)
+        for piece in range(2):
+            gather_start(2, piece)
 
     acc[...] = jnp.zeros_like(acc)
     et[...] = jnp.zeros_like(et)
@@ -291,11 +303,15 @@
     def to_resid(part, target):
         return remote(pout.at[part], resid.at[part], resid_s.at[part], resid_r.at[part], section=target)
 
-    def to_back(target):
-        return remote(back, gbuf.at[0, me], back_s.at[0], back_r.at[0], section=target)
-
-    def to_earlier(target):
-        return remote(gbuf.at[1, me], other, back_s.at[1], back_r.at[1], section=target)
+    def to_back(piece, target):
+        return remote(
+            back.at[piece], gbuf.at[0, piece, me], back_s.at[piece], back_r.at[piece], section=target
+        )
+
+    def to_earlier(piece, target):
+        return remote(
+            gbuf.at[1, piece, me], other.at[piece], back_s.at[2 + piece], back_r.at[2 + piece], section=target
+        )
 
     def to_aide(part, target):
         return remote(mine.at[part], rside, rside_s.at[part], rside_r, section=target)
@@ -367,20 +383,32 @@
 
         @when(jnp.logical_not(last))
         def _():
-            to_back(sibling).wait_recv()
-            gather_start(0)
-            go_sibling(0, me).start()
-
-        @when(aide)
-        def _():
-            to_aide(1, sibling).wait_recv()
-            spread(2, rside[...])
-            finish_loop(2)
-            give_back(2, place + 2)
-
-        @when(jnp.logical_not(last))
-        def _():
-            gather_loop(0)
+            @when(aide)
+            def _():
+                to_aide(1, sibling).wait_recv()
+                spread(2, rside[...])
+
+            for piece in range(2):
+                to_back(piece, sibling).wait_recv()
+                gather_start(0, piece)
+                go_sibling(0, piece, me).start()
+
+            forward(0, 1)
+
+            @when(aide)
+            def _():
+                finish_loop(2)
+                give_back(2, place + 2)
+
+            cross(0, 0)
+            finish(0, 0)
+
+            def step(reach):
+                forward(0, reach)
+                cross(0, reach - 1)
+                finish(0, reach - 1)
+
+            loop(2, line + 1, step)
 
         @when(last)
         def _():
@@ -455,27 +483,31 @@
         def _():
             @when(jnp.logical_not(last))
             def _():
-                go_sibling(0, me).wait_recv()
-                to_earlier(sibling).wait_recv()
-
-            grads = [gbuf[0, me], other[...]]
+                for piece in range(2):
+                    go_sibling(0, piece, me).wait_recv()
+                    to_earlier(piece, sibling).wait_recv()
+
+            grads = [[gbuf[0, piece, me] for piece in range(2)], [other[piece] for piece in range(2)]]
+            spans = [slice(index * quarter, (index + 1) * quarter) for index in range(4)]
             scaled = [
-                (grads[part].astype(f32) * slope[:, cuts[part]]).astype(bf16) for part in range(2)
+                (grads[index // 2][index % 2].astype(f32) * slope[:, spans[index]]).astype(bf16)
+                for index in range(4)
             ]
-            for part in range(2):
-                term = mm(jnp.concatenate(scaled, axis=1), wt[:, cuts[part]])
-                value = (grads[part].astype(f32) + term).astype(bf16)
+            for index in range(4):
+                part, piece = index // 2, index % 2
+                term = mm(jnp.concatenate(scaled, axis=1), wt[:, spans[index]])
+                value = (grads[part][piece].astype(f32) + term).astype(bf16)
                 if part == 0:
-                    back[...] = value
-                    to_back(place - 1).start()
+                    back[piece] = value
+                    to_back(piece, place - 1).start()
                 else:
-                    gbuf[1, me] = value
-                    gather_start(1)
-                    go_sibling(1, me).start()
+                    gbuf[1, piece, me] = value
+                    gather_start(1, piece)
+                    go_sibling(1, piece, me).start()
 
                     @when(depth > 1)
                     def _():
-                        to_earlier(place - 2).start()
+                        to_earlier(piece, place - 2).start()
 
         @when(depth > 0)
         def _():
@@ -510,11 +542,13 @@
 
     @when(is_base & (depth > 0))
     def _():
-        to_back(place - 1).wait_send()
+        for piece in range(2):
+            to_back(piece, place - 1).wait_send()
 
         @when(depth > 1)
         def _():
-            to_earlier(place - 2).wait_send()
+            for piece in range(2):
+                to_earlier(piece, place - 2).wait_send()
 
     @when(jnp.logical_not(last))
     def _():
@@ -526,21 +560,23 @@
 
             @when((is_control, is_base, is_base)[stream] & active[stream])
             def _():
-                @when(d % 2 == across)
-                def _():
-                    @when((d <= me) & (here + 1 < line))
+                for piece in range(2):
+
+                    @when(d % 2 == across)
                     def _():
-                        go_up(stream, d).wait_send()
-
-                    @when((d >= me) & (here > 0))
+                        @when((d <= me) & (here + 1 < line))
+                        def _():
+                            go_up(stream, piece, d).wait_send()
+
+                        @when((d >= me) & (here > 0))
+                        def _():
+                            go_down(stream, piece, d).wait_send()
+
+                        go_across(stream, piece, d).wait_send()
+
+                    @when((d != me) | (jnp.logical_not(last), True, False)[stream])
                     def _():
-                        go_down(stream, d).wait_send()
-
-                    go_across(stream, d).wait_send()
-
-                @when((d != me) | (jnp.logical_not(last), True, False)[stream])
-                def _():
-                    go_sibling(stream, d).wait_send()
+                        go_sibling(stream, piece, d).wait_send()
 
             @when((d > 0) & active[stream])
             def _():
@@ -593,10 +629,10 @@
             pltpu.VMEM((padded, half), bf16),
             pltpu.VMEM((2, padded, half), bf16),
             pltpu.VMEM((2, padded, half), bf16),
-            pltpu.VMEM((padded, half), bf16),
+            pltpu.VMEM((2, padded, half // 2), bf16),
             pltpu.VMEM((padded, width), f32),
-            pltpu.VMEM((3, n_dp, padded, half), bf16),
-            pltpu.VMEM((padded, half), bf16),
+            pltpu.VMEM((3, 2, n_dp, padded, half // 2), bf16),
+            pltpu.VMEM((2, padded, half // 2), bf16),
             pltpu.VMEM((padded, half), bf16),
             pltpu.VMEM((3, n_dp, padded - lanes + share, lanes), bf16),
             pltpu.VMEM((3, n_dp, padded - lanes + share, lanes), bf16),
@@ -604,8 +640,8 @@
             pltpu.VMEM((2, share, half), bf16),
             pltpu.VMEM((share, half), bf16),
             dma((6,)), dma((2,)), dma((2,)), dma((2,)), dma((2,)), dma((2,)), dma((2,)),
-            dma((2,)), dma((2,)), dma((3, n_dp)), dma((3, n_dp)), dma((9, n_dp)), dma((3, n_dp)),
-            dma((3, n_dp)), dma((3, n_dp)), dma((2,)), dma, dma((2,)), dma,
+            dma((4,)), dma((4,)), dma((3, n_dp)), dma((3, n_dp)), dma((18, n_dp)), dma((6, n_dp)),
+            dma((6, n_dp)), dma((6, n_dp)), dma((2,)), dma, dma((2,)), dma,
         ],
         compiler_params=pltpu.CompilerParams(
             collective_id=0, has_side_effects=True, vmem_limit_bytes=56 * 1024 * 1024

time: 53 us -> 50.9 us (0.960)
  Pallas kernels: 50.9 us -> 48.8 us
    pallas_call x1, Pallas kernels: 50.9 us -> 48.8 us  [body(): pl.pallas_call(functools.partial(kernel, blocks, n_dp, grad_scale), out_s...]
where the time goes in v2:
time: 50.9 us; the launch traced here: 50.7 us
  Pallas kernels  48.8 us (96%)
  local copies, waits for them, and re-layouts  1.92 us (4%)
    pallas_call x1, Pallas kernels, body(): pl.pallas_call(functools.partial(kernel, blocks, n_dp, grad_scale), out_s...  48.8 us
    unnamed x1, local copies, waits for them, and re-layouts  1.92 us

profile of v2, /device:TPU:0, one launch (start us, length us, event | category | flops | bytes accessed | tf_op | source)
XLA Modules:
  0.0 50.7 jit_solution(3232122755996162804)
XLA Ops:
  0.0 48.8 %shard_map.64 = f32[1,96,1536]{2,1,0:T(8,128)} custom-call(s32[6]{0:T(128)} %order_any.1, bf16[6,22,1536]{2,1,0:T(8,128)(2,1)} %lat_any.1, bf16[6,22,1536]{2,1,0:T(8,128)(2,1)} %hint_any.1, bf16[6,22,1536]{2,1,0:T(8,128)(2,1)} %up_any.1, bf16[1,1536,1536]{2,1,0:T(8,128)(2,1)} %w_any.1, bf16[1,768,1536]{2,1,0:T(8,128)(2,1)} %z_any.1), custom_call_target="tpu_custom_call" | custom-call | tf_op jit(solution)/shard_map/pallas_call | solution.py:612
  48.8 1.9 %copy.8 = f32[1,96,1536]{2,1,0:T(8,128)} copy(f32[1,96,1536]{2,1,0:T(8,128)} %shard_map.64) | data formatting | bytes 1179648

commit v3 on v2

--- a/solution.py
+++ b/solution.py
@@ -252,9 +252,9 @@
                     ).wait_recv()
 
                 both = jnp.concatenate([gbuf[stream, 0, d], gbuf[stream, 1, d]], axis=1)
-                term = mm(ecol[stream, d, extra:, :], both[:lanes, :])
                 rest = ecol[stream, d, :extra, :].astype(f32).T[:share, :].astype(bf16)
-                acc[stream] += term + mm(rest, both[lanes:, :])
+                left = jnp.concatenate([ecol[stream, d, extra:, :], rest], axis=1)
+                acc[stream] += mm(left, both)
 
         sides(near, job)
 

time: 50.9 us -> 50.8 us (level)
  no operation moved by 1% of the time
where the time goes in v3:
time: 50.8 us; the launch traced here: 50.6 us
  Pallas kernels  48.7 us (96%)
  local copies, waits for them, and re-layouts  1.92 us (4%)
    pallas_call x1, Pallas kernels, body(): pl.pallas_call(functools.partial(kernel, blocks, n_dp, grad_scale), out_s...  48.7 us
    unnamed x1, local copies, waits for them, and re-layouts  1.92 us

profile of v3, /device:TPU:0, one launch (start us, length us, event | category | flops | bytes accessed | tf_op | source)
XLA Modules:
  0.0 50.6 jit_solution(16678129384091319655)
XLA Ops:
  0.0 48.7 %shard_map.64 = f32[1,96,1536]{2,1,0:T(8,128)} custom-call(s32[6]{0:T(128)} %order_any.1, bf16[6,22,1536]{2,1,0:T(8,128)(2,1)} %lat_any.1, bf16[6,22,1536]{2,1,0:T(8,128)(2,1)} %hint_any.1, bf16[6,22,1536]{2,1,0:T(8,128)(2,1)} %up_any.1, bf16[1,1536,1536]{2,1,0:T(8,128)(2,1)} %w_any.1, bf16[1,768,1536]{2,1,0:T(8,128)(2,1)} %z_any.1), custom_call_target="tpu_custom_call" | custom-call | tf_op jit(solution)/shard_map/pallas_call | solution.py:612
  48.7 1.9 %copy.8 = f32[1,96,1536]{2,1,0:T(8,128)} copy(f32[1,96,1536]{2,1,0:T(8,128)} %shard_map.64) | data formatting | bytes 1179648
